TPU v7x, 1024 devices: a whole 8x8x8 slice. The times are simulated.
1024 devices in a mesh: replica: 16 (over x_hi, z), expert: 32 (over y, x_lo), tensor: 2 (over core).
Axes of the slice: x: 8 (x_hi: 2, x_lo: 4; x = x_hi * 4 + x_lo), y: 8, z: 8, core: 2. Of those that a mesh axis runs over, the one named last changes fastest.
Arguments:
- queries: bfloat16 [4, 512, 128, 576], P(None, ('replica', 'expert'), 'tensor'), may hold values from -276 to 276
- latent_cache: bfloat16 [512, 1024, 576], P(('replica', 'expert')), may hold values from -6 to 6
- cache_lengths: int32 [512], P(('replica', 'expert')), may hold values from 1 to 1020, 261120 in all
- hidden_acts: bfloat16 [8192, 2, 2048], P(('replica', 'expert')), may hold values from -6 to 6
- routes: int32 [8192, 2], P(('replica', 'expert')), may hold values from 0 to 31, all different within a row; in each aligned block of 16 rows (0 to 15, 16 to 31, ...) at most 2 rows name the same one
- route_weights: float32 [8192, 2], P(('replica', 'expert')), may hold values from 0.2 to 1
- stored_values: bfloat16 [32, 2048, 7168], P('expert', ('replica', 'tensor')), may hold values from -0.125 to 0.125
- block_scales: float32 [32, 16, 56], P('expert'), may hold values from 0.25 to 4
Outputs:
- attended: bfloat16 [4, 512, 128, 512], P(None, ('replica', 'expert'), 'tensor')
- synced_weights: bfloat16 [32, 2048, 7168], P('expert', None, ('replica', 'tensor'))
- expert_output: bfloat16 [8192, 16, 2, 224], P(('replica', 'expert'), None, 'tensor')
Inputs may be any that keep to these rules, and one draw needn't show every extreme that they name: `routes`: A row names 2 different experts, and no expert is named by more than 2 of the 16 rows of one device. `cache_lengths`: each sequence leaves room for the 4 new tokens; the lengths sum to 261120.
All inputs are finite; a program needn't handle non-finite values. No bound on the sum of `cache_lengths` on one device may be relied on, other than what follows from the above.
Results may differ from a plain program's by a relative error of at most 0.0057.
Values may be sent and summed in bfloat16 or wider, within the bound.
A program may use at most 64 MiB of HBM per device.

v0:
```python
import jax
import jax.numpy as jnp
from jax import lax
from jax.sharding import PartitionSpec as P

ROPE = 64
QB = 128


SCORE_SCALE = 192.0 ** (-0.5)


def attend_one(packed):
    query_block, key_rows, length = packed
    step_count, head_count, full_width = query_block.shape
    positions = key_rows.shape[0]
    flat_query = query_block.reshape(step_count * head_count, full_width)
    scores = lax.dot_general(
        flat_query, key_rows, (((1,), (1,)), ((), ())), preferred_element_type=jnp.float32
    )
    scores = scores.reshape(step_count, head_count, positions) * SCORE_SCALE
    position = lax.broadcasted_iota(jnp.int32, (step_count, 1, positions), 2)
    allowed = length + lax.broadcasted_iota(jnp.int32, (step_count, 1, 1), 0) + 1
    scores = jnp.where(position < allowed, scores, -jnp.inf)
    peak = jnp.max(scores, axis=-1, keepdims=True)
    raised = jnp.exp(scores - peak)
    denominator = jnp.sum(raised, axis=-1, keepdims=True)
    weights = (raised / denominator).astype(jnp.bfloat16)
    latent_width = full_width - ROPE
    mixed_rows = jnp.dot(
        weights.reshape(step_count * head_count, positions),
        key_rows[:, :latent_width],
        preferred_element_type=jnp.float32,
    )
    return mixed_rows.reshape(step_count, head_count, latent_width).astype(jnp.bfloat16)


def local(
    queries,
    latent_cache,
    cache_lengths,
    hidden_acts,
    routes,
    route_weights,
    stored_values,
    block_scales,
):
    attended = lax.map(attend_one, (jnp.moveaxis(queries, 1, 0), latent_cache, cache_lengths))
    attended = jnp.moveaxis(attended, 0, 1)
    arrived_values = lax.all_to_all(
        stored_values, ("replica", "tensor"), split_axis=2, concat_axis=1, tiled=True
    )
    block_width = arrived_values.shape[2]
    hidden_width = arrived_values.shape[1]
    column_blocks = block_scales.shape[2]
    columns = lax.axis_index(("replica", "tensor")) * block_width + lax.iota(jnp.int32, block_width)
    selector = (columns[None, :] // QB == lax.iota(jnp.int32, column_blocks)[:, None]).astype(
        jnp.float32
    )
    row_scales = jnp.repeat(block_scales, QB, axis=1)
    full_scales = jnp.einsum("ehb,bc->ehc", row_scales, selector, precision=lax.Precision.HIGHEST)
    synced_weights = (arrived_values.astype(jnp.float32) * full_scales).astype(jnp.bfloat16)
    tok_rows, route_count = routes.shape
    owners = lax.axis_size("expert")
    replica_count = lax.axis_size("replica")
    capacity = 2 * ((tok_rows * route_count + owners - 1) // owners)
    pair_count = tok_rows * route_count
    flat_routes = routes.reshape(pair_count)
    onehot = (flat_routes[:, None] == lax.iota(jnp.int32, owners)[None, :]).astype(jnp.int32)
    earlier = jnp.cumsum(onehot, axis=0) - onehot
    slot_index = jnp.sum(earlier * onehot, axis=1)
    target = flat_routes * capacity + slot_index
    placer = (target[None, :] == lax.iota(jnp.int32, owners * capacity)[:, None]).astype(
        jnp.bfloat16
    )
    outgoing = jnp.dot(
        placer, hidden_acts.reshape(pair_count, hidden_width), preferred_element_type=jnp.float32
    )
    outgoing = outgoing.astype(jnp.bfloat16).reshape(owners, capacity, hidden_width)
    arrived_rows = lax.all_to_all(outgoing, "expert", split_axis=0, concat_axis=0, tiled=True)
    weight_block = synced_weights[0]
    stacked = arrived_rows.reshape(1, -1, hidden_width)
    product = lax.dot_general(
        lax.all_gather(stacked, "replica", axis=0, tiled=True),
        weight_block,
        (((2,), (0,)), ((), ())),
        preferred_element_type=jnp.float32,
    )
    produced = product.astype(jnp.bfloat16)
    produced = produced.reshape(replica_count, owners, capacity, 1, block_width)
    returned = lax.all_to_all(
        lax.all_to_all(produced, "replica", split_axis=0, concat_axis=3, tiled=True),
        "expert",
        split_axis=1,
        concat_axis=1,
        tiled=True,
    )
    expert_rows = returned.reshape(owners * capacity, replica_count * block_width)
    picked = lax.dot_general(
        placer, expert_rows, (((0,), (0,)), ((), ())), preferred_element_type=jnp.float32
    )
    combined = jnp.sum(
        picked.reshape(tok_rows, route_count, -1) * route_weights[:, :, None], axis=1
    )
    expert_output = combined.astype(jnp.bfloat16).reshape(tok_rows, replica_count, 1, block_width)
    return (attended, synced_weights, expert_output)


def solution(mesh):
    placed = (
        P(None, ("replica", "expert"), "tensor", None),
        P(("replica", "expert"), None, None),
        P(("replica", "expert")),
        P(("replica", "expert"), None, None),
        P(("replica", "expert"), None),
        P(("replica", "expert"), None),
        P("expert", ("replica", "tensor"), None),
        P("expert", None, None),
    )
    return jax.shard_map(
        local,
        mesh=mesh,
        in_specs=placed,
        out_specs=(
            P(None, ("replica", "expert"), "tensor", None),
            P("expert", None, ("replica", "tensor")),
            P(("replica", "expert"), None, "tensor", None),
        ),
        check_vma=False,
    )
```

profile of v0, /device:TPU:1, one launch (start us, length us, event | category | flops | bytes accessed | tf_op | source)
XLA Modules:
  0.0 250.0 jit_solution(17980775523844396237)
XLA Ops:
  7.2 1.0 reshape.161
  8.3 0.8 copy.48
  9.5 0.2 convolution_convert_fusion
  9.7 0.2 reshape.162
  9.9 21.9 %all_to_all.37 = bf16[32,2,2048]{2,1,0:T(2,128)(2,1)S(1)} all-to-all(bf16[32,2,2048]{2,1,0:T(2,128)(2,1)S(1)} %reshape.162), channel_id=1, replica_groups=mesh['replica'=16,'expert'=32,'tensor'=2] {'expert'}, dimensions={0} | all-to-all | bytes 524288 | tf_op jit(solution)/shard_map/all_to_all | solution.py:80
  31.7 0.8 reshape.163
  32.6 6.0 %copy.45 = bf16[1,64,7168]{1,0,2:T(2,128)(2,1)} copy(bf16[1,64,7168]{2,1,0:T(8,128)(2,1)S(1)} %copy-done.3) | data formatting | bytes 1835008 | tf_op args[6]
  38.6 0.5 broadcast.104
  39.1 39.8 %reduce = bf16[7168,64]{1,0:T(8,128)(2,1)S(1)} reduce(bf16[7168,1,64]{2,1,0:T(2,128)(2,1)} %bitcast.55, bf16[]{:T(256)} %broadcast.104), dimensions={1}, to_apply=%bitcast.44.reduce_sub_computation | reduce | bytes 1835010
  78.9 1.8 reshape.173
  80.7 21.9 %all-to-all-start = ((bf16[32,2,7168]{2,1,0:T(2,128)(2,1)}), bf16[32,2,7168]{2,1,0:T(2,128)(2,1)S(1)}, u32[]{:S(2)}, u32[]{:S(2)}) async-start(bf16[32,2,7168]{2,1,0:T(2,128)(2,1)} %reshape.173), calls=%async_computation | async-start | bytes 1835008 | tf_op jit(solution)/shard_map/all_to_all | solution.py:50
  102.6 38.9 %all-to-all-done = bf16[32,2,7168]{2,1,0:T(2,128)(2,1)S(1)} async-done(((bf16[32,2,7168]{2,1,0:T(2,128)(2,1)}), bf16[32,2,7168]{2,1,0:T(2,128)(2,1)S(1)}, u32[]{:S(2)}, u32[]{:S(2)}) %all-to-all-start) | async-done | bytes 917536 | tf_op jit(solution)/shard_map/all_to_all | solution.py:50
  141.5 4.2 %reshape.174 = bf16[7168,1,64]{2,1,0:T(2,128)(2,1)} reshape(bf16[32,2,7168]{2,1,0:T(2,128)(2,1)S(1)} %all-to-all-done) | data formatting | bytes 1835008
  145.7 7.8 %bitcast_convert_fusion = f32[1,64,7168]{1,0,2:T(1,128)} fusion(bf16[7168,1,64]{2,1,0:T(2,128)(2,1)} %reshape.174), kind=kLoop, calls=%fused_computation.41 | loop fusion | flops 458752 | bytes 2752512 | tf_op jit(solution)/shard_map/convert_element_type | solution.py:62
  153.5 2.7 %copy.46 = f32[1,64,32,224]{3,1,2,0:T(8,128)S(1)} copy(f32[1,64,32,224]{1,3,2,0:T(8,128)} %bitcast.54) | data formatting | bytes 3670016 | tf_op jit(solution)/shard_map/convert_element_type | solution.py:62
  156.2 1.8 copy.47
  158.1 2.5 fusion.2
  160.6 32.2 %all-gather.2.cloned.1.call-done = bf16[16,64,2048]{2,1,0:T(8,128)(2,1)} async-done(((bf16[1,64,2048]{2,1,0:T(8,128)(2,1)}), bf16[16,64,2048]{2,1,0:T(8,128)(2,1)}) %all-gather.2.cloned.1.call-update) | async-done | bytes 4194320 | tf_op jit(solution)/shard_map/all_gather | solution.py:84
  192.8 3.5 %convolution_convert_fusion.1 = bf16[16,64,224]{2,1,0:T(8,128)(2,1)S(1)} fusion(bf16[16,64,2048]{2,1,0:T(8,128)(2,1)} %all-gather.2.cloned.1.call-done, bf16[2048,224]{0,1:T(8,128)(2,1)S(1)} %fusion.2), kind=kOutput, calls=%fused_computation.10 | convolution fusion | flops 939753472 | bytes 5570560 | tf_op jit(solution)/shard_map/dot_general | solution.py:83
  196.3 1.0 reshape.164
  197.3 4.9 %all-to-all-start.2 = ((bf16[16,32,2,1,224]{4,2,1,3,0:T(2,128)(2,1)}), bf16[16,32,2,1,224]{4,2,1,3,0:T(2,128)(2,1)S(1)}, u32[]{:S(2)}, u32[]{:S(2)}) async-start(bf16[16,32,2,1,224]{4,2,1,3,0:T(2,128)(2,1)} %bitcast.17), calls=%async_computation.2 | async-start | bytes 1048576 | tf_op jit(solution)/shard_map/all_to_all | solution.py:92
  202.8 12.5 %all-to-all-done.2 = bf16[16,32,2,1,224]{4,2,1,3,0:T(2,128)(2,1)S(1)} async-done(((bf16[16,32,2,1,224]{4,2,1,3,0:T(2,128)(2,1)}), bf16[16,32,2,1,224]{4,2,1,3,0:T(2,128)(2,1)S(1)}, u32[]{:S(2)}, u32[]{:S(2)}) %all-to-all-start.2) | async-done | bytes 458784 | tf_op jit(solution)/shard_map/all_to_all | solution.py:92
  215.3 1.4 copy.51
  216.7 10.4 %all-to-all-start.3 = ((bf16[1,32,2,16,224]{4,2,3,0,1:T(2,128)(2,1)}), bf16[1,32,2,16,224]{4,2,3,0,1:T(2,128)(2,1)S(1)}, u32[]{:S(2)}, u32[]{:S(2)}) async-start(bf16[1,32,2,16,224]{4,2,3,0,1:T(2,128)(2,1)} %copy.51), calls=%async_computation.3 | async-start | bytes 1048576 | tf_op jit(solution)/shard_map/all_to_all | solution.py:91
  227.3 1.5 copy.43
  228.8 0.6 fusion.4
  229.4 0.3 fusion.21
  229.8 2.8 %fusion.8 = bf16[4,1,64,512]{3,2,1,0:T(8,128)(2,1)} fusion(bf16[1024,576]{1,0:T(8,128)(2,1)} %bitcast.59, f32[4,64]{1,0:T(4,128)S(1)} %fusion.21, f32[4,64,1024]{2,1,0:T(8,128)S(1)} %fusion.4), kind=kOutput, calls=%fused_computation.14 | convolution fusion | flops 269354240 | bytes 3409920 | tf_op jit(solution)/shard_map/while/body/eval_jaxpr/dot_general | solution.py:30
  232.5 8.5 %all-to-all-done.3 = bf16[1,32,2,16,224]{4,2,3,0,1:T(2,128)(2,1)S(1)} async-done(((bf16[1,32,2,16,224]{4,2,3,0,1:T(2,128)(2,1)}), bf16[1,32,2,16,224]{4,2,3,0,1:T(2,128)(2,1)S(1)}, u32[]{:S(2)}, u32[]{:S(2)}) %all-to-all-start.3) | async-done | bytes 458784 | tf_op jit(solution)/shard_map/all_to_all | solution.py:91
  241.1 0.9 reshape.171
  242.0 0.3 fusion.6
  242.3 0.9 convert_element_type.63
  (29 shorter events, 0.9 us)
Async XLA Ops:
  7.2 221.7 %copy-start = (bf16[4,1,64,576]{3,2,1,0:T(8,128)(2,1)S(1)}, bf16[4,1,64,576]{3,2,1,0:T(8,128)(2,1)}, u32[]{:S(2)}) copy-start(bf16[4,1,64,576]{3,2,1,0:T(8,128)(2,1)} %param.8) | copy-start | bytes 884740
  7.2 25.4 %copy-start.3 = (bf16[1,64,7168]{2,1,0:T(8,128)(2,1)S(1)}, bf16[1,64,7168]{2,1,0:T(8,128)(2,1)}, u32[]{:S(2)}) copy-start(bf16[1,64,7168]{2,1,0:T(8,128)(2,1)} %param.14) | copy-start | bytes 2752516
  7.2 185.6 %all-gather.2.cloned.1.call-start = ((), (), s32[]{:S(2)}) async-start(), calls=%async_computation.4 | async-start | bytes 4456448 | tf_op jit(solution)/shard_map/all_gather | solution.py:84
  80.7 60.8 %all-to-all-start = ((bf16[32,2,7168]{2,1,0:T(2,128)(2,1)}), bf16[32,2,7168]{2,1,0:T(2,128)(2,1)S(1)}, u32[]{:S(2)}, u32[]{:S(2)}) async-start(bf16[32,2,7168]{2,1,0:T(2,128)(2,1)} %reshape.173), calls=%async_computation | async-start | bytes 1835008 | tf_op jit(solution)/shard_map/all_to_all | solution.py:50
  156.2 1.8 copy-start.4
  160.6 35.7 %copy-start.2 = (bf16[2048,224]{0,1:T(8,128)(2,1)}, bf16[2048,224]{0,1:T(8,128)(2,1)S(1)}, u32[]{:S(2)}) copy-start(bf16[2048,224]{0,1:T(8,128)(2,1)S(1)} %fusion.2) | copy-start | bytes 2752516
  197.3 30.0 %copy-start.1 = (bf16[1,1024,576]{1,2,0:T(8,128)(2,1)S(1)}, bf16[1,1024,576]{1,2,0:T(8,128)(2,1)}, u32[]{:S(2)}) copy-start(bf16[1,1024,576]{1,2,0:T(8,128)(2,1)} %param.9) | copy-start | bytes 3538948
  197.3 18.0 %all-to-all-start.2 = ((bf16[16,32,2,1,224]{4,2,1,3,0:T(2,128)(2,1)}), bf16[16,32,2,1,224]{4,2,1,3,0:T(2,128)(2,1)S(1)}, u32[]{:S(2)}, u32[]{:S(2)}) async-start(bf16[16,32,2,1,224]{4,2,1,3,0:T(2,128)(2,1)} %bitcast.17), calls=%async_computation.2 | async-start | bytes 1048576 | tf_op jit(solution)/shard_map/all_to_all | solution.py:92
  216.7 24.3 %all-to-all-start.3 = ((bf16[1,32,2,16,224]{4,2,3,0,1:T(2,128)(2,1)}), bf16[1,32,2,16,224]{4,2,3,0,1:T(2,128)(2,1)S(1)}, u32[]{:S(2)}, u32[]{:S(2)}) async-start(bf16[1,32,2,16,224]{4,2,3,0,1:T(2,128)(2,1)} %copy.51), calls=%async_computation.3 | async-start | bytes 1048576 | tf_op jit(solution)/shard_map/all_to_all | solution.py:91
  229.8 2.8 %copy-start.5 = (s32[16,2]{0,1:T(2,128)S(1)}, s32[16,2]{0,1:T(2,128)}, u32[]{:S(2)}) copy-start(s32[16,2]{0,1:T(2,128)} %param.12) | copy-start | bytes 388
  232.5 9.4 %copy-start.6 = (f32[16,2]{0,1:T(2,128)S(1)}, f32[16,2]{0,1:T(2,128)}, u32[]{:S(2)}) copy-start(f32[16,2]{0,1:T(2,128)} %param.13) | copy-start | bytes 388
Sparse Core Ops, SparseCore 0:
  32.7 160.0 all-gather.1
where the time goes:
time: 254 us; the launch traced here: 250 us
  waiting for transfers between devices  92.1 us (36%)
  other arithmetic  48.3 us (19%)
  starting transfers between devices  37.2 us (15%)
  local copies, waits for them, and re-layouts  25.9 us (10%)
  blocking collectives  21.9 us (9%)
  between operations  14.9 us (6%)
  matrix products  9.76 us (4%)
    unnamed x1, other arithmetic  39.8 us
    all_to_all x1, waiting for transfers between devices, local(): lax.all_to_all(stored_values, ('replica', 'tensor'), split_axis=2, concat...  38.9 us
    all_gather x1, waiting for transfers between devices, local(): lax.all_gather(stacked, 'replica', axis=0, tiled=True)  32.2 us
    all_to_all x1, starting transfers between devices, local(): lax.all_to_all(stored_values, ('replica', 'tensor'), split_axis=2, concat...  21.9 us
    all_to_all x1, blocking collectives, local(): lax.all_to_all(outgoing, 'expert', split_axis=0, concat_axis=0, tiled=True)  21.9 us
    unnamed x20, local copies, waits for them, and re-layouts  14.8 us
    all_to_all x1, waiting for transfers between devices, local(): lax.all_to_all(produced, 'replica', split_axis=0, concat_axis=3, tiled=True)  12.5 us
    all_to_all x1, starting transfers between devices, local(): lax.all_to_all(lax.all_to_all(produced, 'replica', split_axis=0, concat_a...  10.4 us
  transfers between devices with their start and end apart: 4, of which 4 were waited for; matrix products, arithmetic and copies ran while one was open for 29% of the time, Pallas kernels for 0%

commit v1 on v0

v1 whole, which is shorter than its diff:
```python
import functools

import jax
import jax.numpy as jnp
from jax import lax
from jax.experimental import pallas as pl
from jax.experimental.pallas import tpu as pltpu
from jax.sharding import PartitionSpec as P

XH = 2
XL = 4
SLOTS = 2
QB = 128
ROPE = 64
SCORE_SCALE = 192.0 ** (-0.5)
LANES = 128
MESH = pl.DeviceIdType.MESH
F32 = jnp.float32
BF16 = jnp.bfloat16


def iota(shape, axis):
    return lax.broadcasted_iota(jnp.int32, shape, axis)


def onehot(mask):
    return jnp.where(mask, 1.0, 0.0).astype(BF16)


def kernel(
    sizes,
    lengths,
    scales,
    routes,
    weights,
    hidden,
    queries,
    cache,
    stored,
    attended,
    synced,
    gathered,
    pack_out,
    pack_in,
    wfull,
    stacked,
    y_out,
    y_in,
    x_out,
    rows,
    products,
    r_out,
    r_in,
    meta,
    f_out,
    f_in,
    perm,
    att,
    local_sem,
    send_sem,
    w_sem,
    y_sem,
    x_sem,
    right_sem,
    left_sem,
    pair_sem,
    meta_sem,
    r_sem,
    f_sem,
):
    nr, ne, nt = sizes
    nz, ny = nr // XH, ne // XL
    nx = XH * XL
    tok = routes.shape[0]
    width = stored.shape[1] // (nr * nt)
    depth = stored.shape[0]
    chunks = hidden.shape[1] // (2 * nt * LANES)
    half = chunks * LANES
    groups = max(1, nz // 4)
    per = nz // groups
    order = [0]
    for step in range(1, nz // 2):
        order += [-step, step]
    order.append(nz // 2)

    r, e, t = lax.axis_index("replica"), lax.axis_index("expert"), lax.axis_index("tensor")
    xh, z = r // nz, r % nz
    y, xl = e // XL, e % XL
    x = xh * XL + xl
    me = r * nt + t

    def to(rep, exp, ten):
        return {"replica": rep, "expert": exp, "tensor": ten}

    barrier = pltpu.get_barrier_semaphore()

    def greet(rep, exp, ten):
        pl.semaphore_signal(barrier, inc=1, device_id=to(rep, exp, ten), device_id_type=MESH)

    @pl.loop(1, nr * nt)
    def _(d):
        other = (me + d) % (nr * nt)
        greet(other // nt, e, other % nt)

    @pl.loop(1, ne)
    def _(d):
        greet(r, (e + d) % ne, t)

    for dh in range(1, XH):
        for dl in range(1, XL):
            greet((xh + dh) % XH * nz + z, y * XL + (xl + dl) % XL, t)

    named = routes[...].astype(F32)
    column = [named[:, k : k + 1] for k in range(2)]
    eye = iota((tok, tok), 0) == iota((tok, tok), 1)
    before = iota((tok, tok), 1) < iota((tok, tok), 0)
    line = [jnp.sum(jnp.where(eye, c, 0.0), axis=0, keepdims=True) for c in column]
    slot = []
    for k in range(2):
        count = jnp.sum(jnp.where((column[k] == line[k]) & before, 1.0, 0.0), axis=1, keepdims=True)
        for other in range(k):
            count += jnp.sum(jnp.where(column[k] == line[other], 1.0, 0.0), axis=1, keepdims=True)
        slot.append(count)
    pairs = 2 * tok
    block = chunks * SLOTS
    target = jnp.concatenate([column[k] * block + slot[k] for k in range(2)], axis=0)
    lane = iota((pairs, chunks * pairs), 1)
    spread = jnp.where(lane % pairs == iota((pairs, chunks * pairs), 0), target, 0.0)
    wanted = jnp.sum(spread, axis=0, keepdims=True)
    wanted = wanted + (iota((1, chunks * pairs), 1) // pairs * SLOTS).astype(F32)
    placer = onehot(iota((ne * block, chunks * pairs), 0).astype(F32) == wanted)
    for c in range(chunks):
        for k in range(2):
            start = pl.multiple_of(k * nt * half + t * half + c * LANES, LANES)
            stacked[c * pairs + k * tok : c * pairs + (k + 1) * tok, :] = hidden[:, pl.ds(start, LANES)]
    y_out[...] = (
        jnp.dot(placer, stacked[...], preferred_element_type=F32).astype(BF16).reshape(y_out.shape)
    )
    lane = iota((tok, LANES), 1)
    note = jnp.zeros((tok, LANES), F32)
    for k in range(2):
        place = column[k] * (nz * XH * SLOTS) + slot[k]
        note = jnp.where(lane == k, place, note)
        note = jnp.where(lane == 2 + k, weights[:, k : k + 1], note)
    meta[r] = note

    pl.semaphore_wait(barrier, nr * nt - 1 + ne - 1 + (XH - 1) * (XL - 1))

    @pl.loop(1, ny)
    def _(d):
        other = (y + d) % ny
        pltpu.make_async_remote_copy(
            y_out.at[other], y_in.at[y], send_sem.at[0], y_sem,
            device_id=to(r, other * XL + xl, t), device_id_type=MESH,
        ).start()

    own = pltpu.make_async_copy(y_out.at[y], y_in.at[y], local_sem.at[0])
    own.start()

    @pl.loop(1, nr)
    def _(d):
        other = (r + d) % nr
        pltpu.make_async_remote_copy(
            meta.at[r], meta.at[r], send_sem.at[1], meta_sem,
            device_id=to(other, e, t), device_id_type=MESH,
        ).start()

    window = 4 * width
    tiles = window // QB
    part = depth // 4

    @pl.loop(0, nr * nt // 4)
    def _(q):
        values = stored[:, pl.ds(pl.multiple_of(q * window, QB), window)].astype(F32)
        row = me * depth // QB
        values = jnp.concatenate(
            [values[:, j * QB : (j + 1) * QB] * scales[row, q * tiles + j] for j in range(tiles)], axis=1
        ).astype(BF16)
        for b in range(4):
            pack_out[q * 4 + b] = jnp.concatenate(
                [values[part * g : part * (g + 1), width * b : width * (b + 1)] for g in range(4)], axis=1
            )

    @pl.loop(1, nr * nt)
    def _(d):
        other = (me + d) % (nr * nt)
        pltpu.make_async_remote_copy(
            pack_out.at[other], pack_in.at[me], send_sem.at[2], w_sem,
            device_id=to(other // nt, e, other % nt), device_id_type=MESH,
        ).start()

    mine = pltpu.make_async_copy(pack_out.at[me], pack_in.at[me], local_sem.at[1])
    mine.start()

    own.wait()
    pltpu.make_async_copy(y_out.at[pl.ds(0, ny - 1)], y_in.at[pl.ds(0, ny - 1)], y_sem).wait()
    size = ny * block
    out_row, in_row = iota((size, size), 0), iota((size, size), 1)
    source = (out_row // SLOTS) % ny * block + out_row // (ny * SLOTS) * SLOTS + out_row % SLOTS
    turned = jnp.concatenate(
        [
            jnp.concatenate([y_in[k, l * block : (l + 1) * block, :] for k in range(ny)], axis=0)
            for l in range(XL)
        ],
        axis=1,
    )
    turned = jnp.dot(onehot(source == in_row), turned, preferred_element_type=F32).astype(BF16)
    for l in range(XL):
        x_out[l] = turned[:, l * LANES : (l + 1) * LANES]

    @pl.loop(1, nx)
    def _(d):
        other = (x + d) % nx
        pltpu.make_async_remote_copy(
            x_out.at[other % XL], rows.at[z, t, x], send_sem.at[3], x_sem,
            device_id=to(other // XL * nz + z, y * XL + other % XL, t), device_id_type=MESH,
        ).start()

    kept = pltpu.make_async_copy(x_out.at[xl], rows.at[z, t, x], local_sem.at[2])
    kept.start()

    steps, heads, full = queries.shape
    positions = cache.shape[0]
    scores = lax.dot_general(
        queries[...].reshape(steps * heads, full), cache[...], (((1,), (1,)), ((), ())),
        preferred_element_type=F32,
    )
    position = iota((heads, positions), 1)
    for s in range(steps):
        seen = jnp.where(
            position < lengths[0] + s + 1, scores[s * heads : (s + 1) * heads] * SCORE_SCALE, -jnp.inf
        )
        raised = jnp.exp(seen - jnp.max(seen, axis=-1, keepdims=True))
        shares = (raised / jnp.sum(raised, axis=-1, keepdims=True)).astype(BF16)
        att[s] = jnp.dot(shares, cache[:, : full - ROPE], preferred_element_type=F32).astype(BF16)
    attended_copy = pltpu.make_async_copy(att, attended, local_sem.at[3])
    attended_copy.start()

    size = per * nx * ny * SLOTS
    out_row, in_row = iota((size, 1), 0), iota((size, size), 1)
    piece = per * XH * SLOTS
    home, rest = out_row // piece, out_row % piece
    source = (
        rest // (XH * SLOTS) * (nx * ny * SLOTS)
        + (rest // SLOTS % XH * XL + home % XL) * (ny * SLOTS)
        + home // XL * SLOTS
        + rest % SLOTS
    )
    perm[...] = onehot(source == in_row)

    kept.wait()
    pltpu.make_async_copy(rows.at[0, 0, pl.ds(0, nx - 1)], rows.at[0, 0, pl.ds(0, nx - 1)], x_sem).wait()
    hx = nx // 2

    def piece_of(offset, h):
        return rows.at[(z + offset + nz) % nz, t, pl.ds(h * hx, hx)]

    def ring(offset, h, sem, direction):
        copy = pltpu.make_async_remote_copy(
            piece_of(offset, h), piece_of(offset, h), send_sem.at[4], sem,
            device_id=to(xh * nz + (z + direction + nz) % nz, e, t), device_id_type=MESH,
        )
        return copy

    def pair(index, h):
        return pltpu.make_async_remote_copy(
            piece_of(order[index], h), piece_of(order[index], h), send_sem.at[5], pair_sem.at[index, h],
            device_id=to(r, e, 1 - t), device_id_type=MESH,
        )

    def product(index):
        chunk = rows.at[(z + order[index] + nz) % nz]
        left = jnp.concatenate(
            [
                chunk[u, :, c * ny * SLOTS : (c + 1) * ny * SLOTS, :].reshape(nx * ny * SLOTS, LANES)
                for u in range(nt)
                for c in range(chunks)
            ],
            axis=1,
        )
        value = jnp.dot(left, wfull[...], preferred_element_type=F32).astype(BF16)
        where = index % per * (nx * ny * SLOTS)
        products[where : where + nx * ny * SLOTS, :width] = value

    def unpack():
        mine.wait()
        pltpu.make_async_copy(
            pack_out.at[pl.ds(0, nr * nt - 1)], pack_in.at[pl.ds(0, nr * nt - 1)], w_sem
        ).wait()

        @pl.loop(0, nr * nt)
        def _(s):
            values = pack_in[s]
            for g in range(4):
                start = pl.multiple_of(s * depth + g * part, part)
                wfull[pl.ds(start, part), :] = values[:, width * g : width * (g + 1)]

    def send_back(group):
        value = jnp.dot(perm[...], products[...], preferred_element_type=F32).astype(BF16)
        r_out[group] = value.reshape(r_out.shape[1:])

        @pl.loop(1, ne)
        def _(d):
            other = (e + d) % ne
            pltpu.make_async_remote_copy(
                r_out.at[group, other], r_in.at[group, e], send_sem.at[6], r_sem.at[group],
                device_id=to(r, other, t), device_id_type=MESH,
            ).start()

        here = pltpu.make_async_copy(r_out.at[group, e], r_in.at[group, e], local_sem.at[5])
        here.start()
        here.wait()

    products[...] = jnp.zeros_like(products)
    last = nz // 2
    synced_copy = pltpu.make_async_copy(wfull, synced, local_sem.at[4])
    for step in range(last + 1):
        if step == 0:
            for h in range(2):
                ring(0, h, right_sem.at[0, h], 1).start()
                ring(0, h, left_sem.at[0, h], -1).start()
            for h in range(2):
                pair(0, h).start()
        else:
            for h in range(2):
                if step < last or h == 0:
                    ring(-step, h, right_sem.at[step - 1, h], 1).wait_recv()
                    if step + 1 < last or (step + 1 == last and h == 0):
                        ring(-step, h, right_sem.at[step, h], 1).start()
                    pair(2 * step - 1, h).start()
                if step < last or h == 1:
                    ring(step, h, left_sem.at[step - 1, h], -1).wait_recv()
                    if step + 1 < last or (step + 1 == last and h == 1):
                        ring(step, h, left_sem.at[step, h], -1).start()
                    pair(2 * step if step < last else 2 * step - 1, h).start()
        if step == 0:
            unpack()
            synced_copy.start()
        ready = [0] if step == 0 else [2 * step - 1, 2 * step] if step < last else [2 * step - 1]
        for index in ready:
            for h in range(2):
                pair(index, h).wait_recv()
            product(index)
            if index % per == per - 1:
                send_back(index // per)

    pltpu.make_async_copy(meta.at[pl.ds(0, nr - 1)], meta.at[pl.ds(0, nr - 1)], meta_sem).wait()
    for group in range(groups):
        pltpu.make_async_copy(
            r_out.at[group, pl.ds(0, ne - 1)], r_in.at[group, pl.ds(0, ne - 1)], r_sem.at[group]
        ).wait()
    arrived = [r_in[group].reshape(ne * piece, r_in.shape[-1]) for group in range(groups)]
    position = iota((tok, ne * piece), 1).astype(F32)
    for index in range(nz):
        group = index // per
        for h in range(XH):
            home = h * nz + (z + order[index] + nz) % nz
            facts = meta[home]
            total = jnp.zeros((tok, r_in.shape[-1]), F32)
            picks = []
            for k in range(2):
                place = facts[:, k : k + 1]
                place = jnp.floor(place * (1.0 / (nz * XH * SLOTS))) * piece + (
                    place - jnp.floor(place * (1.0 / (nz * XH * SLOTS))) * (nz * XH * SLOTS)
                )
                place = place + (index % per * XH * SLOTS + h * SLOTS)
                picks.append(onehot(position == place))
            picked = jnp.dot(jnp.concatenate(picks, axis=0), arrived[group], preferred_element_type=F32)
            for k in range(2):
                total += picked[k * tok : (k + 1) * tok] * facts[:, 2 + k : 3 + k]
            f_out[home] = total.astype(BF16)

    @pl.loop(1, nr)
    def _(d):
        other = (r + d) % nr
        pltpu.make_async_remote_copy(
            f_out.at[other], f_in.at[r], send_sem.at[7], f_sem,
            device_id=to(other, e, t), device_id_type=MESH,
        ).start()

    final = pltpu.make_async_copy(f_out.at[r], f_in.at[r], local_sem.at[0])
    final.start()
    final.wait()

    def sent(ref, number):
        pltpu.make_async_copy(ref, ref, send_sem.at[number]).wait()

    sent(y_out.at[pl.ds(0, ny - 1)], 0)
    sent(meta.at[pl.ds(0, nr - 1)], 1)
    sent(pack_out.at[pl.ds(0, nr * nt - 1)], 2)
    sent(rows.at[0, 0, pl.ds(0, nx - 1)], 3)
    sent(rows.at[pl.ds(0, nz - 1), 0], 4)
    sent(rows.at[:, 0], 5)
    for group in range(groups):
        sent(r_out.at[group, pl.ds(0, ne - 1)], 6)
    sent(f_out.at[pl.ds(0, nr - 1)], 7)
    attended_copy.wait()
    synced_copy.wait()
    pltpu.make_async_copy(f_out.at[pl.ds(0, nr - 1)], f_in.at[pl.ds(0, nr - 1)], f_sem).wait()
    done = pltpu.make_async_copy(f_in, gathered, local_sem.at[1])
    done.start()
    done.wait()


def local(sizes, queries, latent_cache, cache_lengths, hidden_acts, routes, route_weights, stored_values, block_scales):
    nr, ne, nt = sizes
    nz, ny, nx = nr // XH, ne // XL, XH * XL
    steps, _, heads, full = queries.shape
    tok, _, ffn = hidden_acts.shape
    depth, columns = stored_values.shape[1:]
    width = columns // (nr * nt)
    padded = -(-width // LANES) * LANES
    chunks = ffn // (nt * LANES)
    block = chunks * SLOTS
    groups = max(1, nz // 4)
    per = nz // groups
    piece = per * XH * SLOTS
    size = nx * ny * SLOTS
    vmem = pl.BlockSpec(memory_space=pltpu.VMEM)
    smem = pl.BlockSpec(memory_space=pltpu.SMEM)
    hbm = pl.BlockSpec(memory_space=pl.ANY)
    dma = pltpu.SemaphoreType.DMA
    attended, synced, gathered = pl.pallas_call(
        functools.partial(kernel, sizes),
        out_shape=[
            jax.ShapeDtypeStruct((steps, heads, full - ROPE), BF16),
            jax.ShapeDtypeStruct((ffn, width), BF16),
            jax.ShapeDtypeStruct((nr, tok, padded), BF16),
        ],
        in_specs=[smem, smem, vmem, vmem, vmem, vmem, vmem, vmem],
        out_specs=[hbm, hbm, hbm],
        scratch_shapes=[
            pltpu.VMEM((nr * nt, depth // 4, 4 * width), BF16),
            pltpu.VMEM((nr * nt, depth // 4, 4 * width), BF16),
            pltpu.VMEM((ffn, width), BF16),
            pltpu.VMEM((chunks * 2 * tok, LANES), BF16),
            pltpu.VMEM((ny, XL * block, LANES), BF16),
            pltpu.VMEM((ny, XL * block, LANES), BF16),
            pltpu.VMEM((XL, ny * block, LANES), BF16),
            pltpu.VMEM((nz, nt, nx, ny * block, LANES), BF16),
            pltpu.VMEM((per * size, padded), BF16),
            pltpu.VMEM((groups, ne, piece, padded), BF16),
            pltpu.VMEM((groups, ne, piece, padded), BF16),
            pltpu.VMEM((nr, tok, LANES), F32),
            pltpu.VMEM((nr, tok, padded), BF16),
            pltpu.VMEM((nr, tok, padded), BF16),
            pltpu.VMEM((per * size, per * size), BF16),
            pltpu.VMEM((steps, heads, full - ROPE), BF16),
            dma((6,)),
            dma((8,)),
            dma,
            dma,
            dma,
            dma((nz // 2, 2)),
            dma((nz // 2, 2)),
            dma((nz, 2)),
            dma,
            dma((groups,)),
            dma,
        ],
        compiler_params=pltpu.CompilerParams(
            collective_id=0, has_side_effects=True, vmem_limit_bytes=56 * 1024 * 1024
        ),
        cost_estimate=pl.CostEstimate(flops=2_000_000_000, bytes_accessed=6_000_000, transcendentals=262144),
    )(
        cache_lengths,
        block_scales[0],
        routes,
        route_weights,
        hidden_acts.reshape(tok, 2 * ffn),
        queries.reshape(steps, heads, full),
        latent_cache[0],
        stored_values[0],
    )
    expert_output = jnp.transpose(gathered[:, :, :width], (1, 0, 2)).reshape(tok, nr, 1, width)
    return attended.reshape(steps, 1, heads, full - ROPE), synced[None], expert_output


def solution(mesh):
    sizes = (mesh.shape["replica"], mesh.shape["expert"], mesh.shape["tensor"])
    placed = (
        P(None, ("replica", "expert"), "tensor", None),
        P(("replica", "expert"), None, None),
        P(("replica", "expert")),
        P(("replica", "expert"), None, None),
        P(("replica", "expert"), None),
        P(("replica", "expert"), None),
        P("expert", ("replica", "tensor"), None),
        P("expert", None, None),
    )
    return jax.shard_map(
        functools.partial(local, sizes),
        mesh=mesh,
        in_specs=placed,
        out_specs=(
            P(None, ("replica", "expert"), "tensor", None),
            P("expert", None, ("replica", "tensor")),
            P(("replica", "expert"), None, "tensor", None),
        ),
        check_vma=False,
    )
```

time: 254 us -> 116 us (0.46); the launches traced: 250 us -> 115 us
  Pallas kernels: 0 us -> 104 us
  waiting for transfers between devices: 92.1 us -> 0 us
  other arithmetic: 48.3 us -> 0 us
  starting transfers between devices: 37.2 us -> 0 us
  blocking collectives: 21.9 us -> 0 us
  local copies, waits for them, and re-layouts: 25.9 us -> 10.4 us
  between operations: 14.9 us -> 1.31 us
  matrix products: 9.76 us -> 0 us
    pallas_call x0 -> x1, Pallas kernels: none -> 104 us  [local(): pl.pallas_call(functools.partial(kernel, sizes), out_shape=[jax.ShapeDtyp...]
    all_to_all x3 -> x0, waiting for transfers between devices: 59.9 us -> none  [the longest x1 38.9 us: local(): lax.all_to_all(stored_values, ('replica', 'tensor'), split_axis=2, concat...]
    unnamed x1 -> x0, other arithmetic: 39.8 us -> none
    all_to_all x3 -> x0, starting transfers between devices: 37.2 us -> none  [the longest x1 21.9 us: local(): lax.all_to_all(stored_values, ('replica', 'tensor'), split_axis=2, concat...]
    all_gather x1 -> x0, waiting for transfers between devices: 32.2 us -> none  [local(): lax.all_gather(stacked, 'replica', axis=0, tiled=True)]
    all_to_all x1 -> x0, blocking collectives: 21.9 us -> none  [local(): lax.all_to_all(outgoing, 'expert', split_axis=0, concat_axis=0, tiled=True)]
    dot_general x6 -> x0, matrix products: 9.76 us -> none  [the longest x1 3.47 us: local(): lax.dot_general(lax.all_gather(stacked, 'replica', axis=0, tiled=True), w...]
    convert_element_type x2 -> x0, other arithmetic: 7.85 us -> none  [the longest x1 7.78 us: local(): arrived_values.astype(jnp.float32) * full_scales]
  transfers between devices with their start and end apart: 4 -> 0, of which waited for: 4 -> 0; matrix products, arithmetic and copies ran while one was open for 29% -> 0% of each run, Pallas kernels for 0% -> 0%
where the time goes in v1:
time: 116 us; the launch traced here: 115 us
  Pallas kernels  104 us (90%)
  local copies, waits for them, and re-layouts  10.4 us (9%)
  between operations  1.31 us (1%)
    pallas_call x1, Pallas kernels, local(): pl.pallas_call(functools.partial(kernel, sizes), out_shape=[jax.ShapeDtyp...  104 us
    unnamed x11, local copies, waits for them, and re-layouts  10.4 us

profile of v1, /device:TPU:1, one launch (start us, length us, event | category | flops | bytes accessed | tf_op | source)
XLA Modules:
  0.0 115.4 jit_solution(6069188111715675215)
XLA Ops:
  1.3 1.4 %copy.12.routes = s32[16,2]{1,0:T(8,128)} copy(s32[16,2]{0,1:T(2,128)} %param.12) | data formatting | bytes 256 | tf_op args[4]
  2.6 1.4 %copy.13.weights = f32[16,2]{1,0:T(8,128)} copy(f32[16,2]{0,1:T(2,128)} %param.13) | data formatting | bytes 256 | tf_op args[5]
  4.0 1.6 %copy.17 = bf16[2,8,2,2048]{3,1,2,0:T(8,128)(2,1)} copy(bf16[2,8,2,2048]{3,2,1,0:T(2,128)(2,1)} %bitcast.17) | data formatting | bytes 262144
  5.6 2.4 %copy.11 = bf16[1,1024,576]{2,1,0:T(8,128)(2,1)} copy(bf16[1,1024,576]{1,2,0:T(8,128)(2,1)} %param.9) | data formatting | bytes 2359296 | tf_op args[1]
  8.0 103.7 %shard_map.103 = (bf16[4,64,512]{2,1,0:T(8,128)(2,1)}, bf16[2048,224]{1,0:T(8,128)(2,1)}, bf16[16,16,256]{2,1,0:T(8,128)(2,1)}) custom-call(s32[1]{0:T(128)S(6)} %copy.19.lengths, f32[16,56]{1,0:T(8,128)} %bitcast.21, s32[16,2]{1,0:T(8,128)} %copy.12.routes, f32[16,2]{1,0:T(8,128)} %copy.13.weights, bf16[16,4096]{1,0:T(8,128)(2,1)} %bitcast.18, ...), custom_call_target="tpu_custom_call" | custom-call | flops 2000000000 | bytes 6000000 | tf_op jit(solution)/shard_map/pallas_call | solution.py:423
  111.7 0.0 copy-start.1
  111.7 0.0 copy-start
  111.7 2.3 %copy.15 = bf16[1,2048,224]{1,2,0:T(8,128)(2,1)} copy(bf16[1,2048,224]{2,1,0:T(8,128)(2,1)} %bitcast.15) | data formatting | bytes 1835008
  114.0 0.0 copy-done.1
  114.0 0.7 copy.16
  114.7 0.0 copy-done
  114.7 0.7 copy.20
  (1 shorter events, 0.0 us)
Async XLA Ops:
  111.7 2.3 %copy-start.1 = (bf16[16,16,256]{2,1,0:T(8,128)(2,1)S(1)}, bf16[16,16,256]{2,1,0:T(8,128)(2,1)}, u32[]{:S(2)}) copy-start(bf16[16,16,256]{2,1,0:T(8,128)(2,1)} %get-tuple-element.8) | copy-start | bytes 393220
  111.7 3.0 %copy-start = (bf16[4,64,512]{2,1,0:T(8,128)(2,1)S(1)}, bf16[4,64,512]{2,1,0:T(8,128)(2,1)}, u32[]{:S(2)}) copy-start(bf16[4,64,512]{2,1,0:T(8,128)(2,1)} %get-tuple-element.6) | copy-start | bytes 786436

commit v2 on v1

v2 whole, which is shorter than its diff:
```python
import functools

import jax
import jax.numpy as jnp
from jax import lax
from jax.experimental import pallas as pl
from jax.experimental.pallas import tpu as pltpu
from jax.sharding import PartitionSpec as P

XH = 2
XL = 4
SLOTS = 2
QB = 128
ROPE = 64
SCORE_SCALE = 192.0 ** (-0.5)
LANES = 128
PER = 2
MESH = pl.DeviceIdType.MESH
F32 = jnp.float32
BF16 = jnp.bfloat16


def iota(shape, axis):
    return lax.broadcasted_iota(jnp.int32, shape, axis)


def log2(n):
    return n.bit_length() - 1


def onehot(mask):
    return jnp.where(mask, 1.0, 0.0).astype(BF16)


def settle(ref, sem):
    pltpu.make_async_copy(ref, ref, sem).wait()


def kernel(
    sizes,
    lengths,
    scales,
    routes,
    weights,
    hidden,
    queries,
    cache,
    stored,
    attended,
    synced,
    gathered,
    pack_out,
    pack_in,
    wfull,
    stacked,
    y_out,
    y_in,
    x_out,
    rows,
    products,
    r_out,
    r_in,
    meta,
    pick,
    gains,
    f_out,
    f_in,
    final,
    perm,
    scores,
    att,
    local_sem,
    send_sem,
    w_sem,
    y_sem,
    x_sem,
    right_sem,
    left_sem,
    pair_sem,
    meta_sem,
    r_sem,
    f_sem,
):
    nr, ne, nt = sizes
    nz, ny = nr // XH, ne // XL
    nx = XH * XL
    tok = routes.shape[1]
    depth = stored.shape[0]
    width = stored.shape[1] // (nr * nt)
    chunks = hidden.shape[2] // (nt * LANES)
    half = chunks * LANES
    groups = nz // PER
    per = PER
    block = chunks * SLOTS
    line_rows = ny * SLOTS
    chunk_rows = nx * line_rows
    piece = per * XH * SLOTS
    halves = products.shape[1] // LANES
    order = [0]
    for step in range(1, nz // 2):
        order += [-step, step]
    order.append(nz // 2)

    r, e, t = lax.axis_index("replica"), lax.axis_index("expert"), lax.axis_index("tensor")
    xh, z = r // nz, r % nz
    y, xl = e // XL, e % XL
    x = xh * XL + xl
    me = r * nt + t

    def to(rep, exp, ten):
        return {"replica": rep, "expert": exp, "tensor": ten}

    def remote(src, dst, send, recv, target):
        return pltpu.make_async_remote_copy(
            src, dst, send_sem.at[send], recv, device_id=target, device_id_type=MESH
        )

    barrier = pltpu.get_barrier_semaphore()

    def greet(rep, exp, ten):
        pl.semaphore_signal(barrier, inc=1, device_id=to(rep, exp, ten), device_id_type=MESH)

    @pl.loop(1, nr * nt)
    def _(d):
        other = (me + d) % (nr * nt)
        greet(other // nt, e, other % nt)

    @pl.loop(1, ne)
    def _(d):
        greet(r, (e + d) % ne, t)

    for dh in range(1, XH):
        for dl in range(1, XL):
            greet((xh + dh) % XH * nz + z, y * XL + (xl + dl) % XL, t)

    named = routes[...].astype(F32)
    line = [named[k : k + 1, :] for k in range(2)]
    eye = iota((tok, tok), 0) == iota((tok, tok), 1)
    before = iota((tok, tok), 1) < iota((tok, tok), 0)
    column = [jnp.sum(jnp.where(eye, v, 0.0), axis=1, keepdims=True) for v in line]
    gain = [jnp.sum(jnp.where(eye, weights[k : k + 1, :], 0.0), axis=1, keepdims=True) for k in range(2)]
    slot = []
    for k in range(2):
        count = jnp.sum(jnp.where((column[k] == line[k]) & before, 1.0, 0.0), axis=1, keepdims=True)
        for other in range(k):
            count += jnp.sum(jnp.where(column[k] == line[other], 1.0, 0.0), axis=1, keepdims=True)
        slot.append(count)
    pairs = 2 * tok
    target = jnp.concatenate([column[k] * block + slot[k] for k in range(2)], axis=0)
    lane = iota((pairs, chunks * pairs), 1)
    spread = jnp.where((lane & (pairs - 1)) == iota((pairs, chunks * pairs), 0), target, 0.0)
    wanted = jnp.sum(spread, axis=0, keepdims=True)
    wanted = wanted + ((iota((1, chunks * pairs), 1) >> log2(pairs)) * SLOTS).astype(F32)
    placer = onehot(iota((ne * block, chunks * pairs), 0).astype(F32) == wanted)
    for c in range(chunks):
        start = pl.multiple_of(t * half + c * LANES, LANES)
        part = hidden[:, :, pl.ds(start, LANES)]
        for k in range(2):
            stacked[c * pairs + k * tok : c * pairs + (k + 1) * tok, :] = part[:, k, :]
    y_out[...] = (
        jnp.dot(placer, stacked[...], preferred_element_type=F32).astype(BF16).reshape(y_out.shape)
    )
    lane = iota((tok, LANES), 1)
    note = jnp.zeros((tok, LANES), F32)
    for k in range(2):
        note = jnp.where(lane == k, column[k] * piece + slot[k], note)
        note = jnp.where(lane == 2 + k, gain[k], note)
    meta[r] = note

    window = 4 * width
    tiles = window // QB
    high = width // 2

    @pl.loop(0, nr * nt // 4)
    def _(q):
        values = stored[:, pl.ds(pl.multiple_of(q * window, QB), window)].astype(F32)
        row = me * depth // QB
        values = jnp.concatenate(
            [values[:, j * QB : (j + 1) * QB] * scales[row, q * tiles + j] for j in range(tiles)], axis=1
        ).astype(BF16)
        values = values.T
        for b in range(4):
            pack_out[q * 4 + b] = jnp.concatenate(
                [values[width * b + high * g : width * b + high * (g + 1), :] for g in range(2)], axis=1
            )

    pl.semaphore_wait(barrier, nr * nt - 1 + ne - 1 + (XH - 1) * (XL - 1))

    @pl.loop(1, ny)
    def _(d):
        other = (y + d) % ny
        remote(y_out.at[other], y_in.at[y], 0, y_sem, to(r, other * XL + xl, t)).start()

    own = pltpu.make_async_copy(y_out.at[y], y_in.at[y], local_sem.at[0])
    own.start()

    def send_weights(first, end):
        @pl.loop(first, end)
        def _(d):
            other = (me + d) % (nz * nt) + (xh + d // (nz * nt)) % XH * (nz * nt)
            remote(pack_out.at[other], pack_in.at[me], 2, w_sem, to(other // nt, e, other % nt)).start()

    send_weights(1, nz * nt)
    mine = pltpu.make_async_copy(pack_out.at[me], pack_in.at[me], local_sem.at[1])
    mine.start()

    size = ny * block
    out_row, in_row = iota((size, 1), 0), iota((size, size), 1)
    source = (
        ((out_row >> log2(SLOTS)) & (ny - 1)) * block
        + (out_row >> log2(line_rows)) * SLOTS
        + (out_row & (SLOTS - 1))
    )
    turn = onehot(source == in_row)
    own.wait()
    settle(y_in.at[pl.ds(0, ny - 1)], y_sem)
    turned = jnp.concatenate(
        [
            jnp.concatenate([y_in[k, l * block : (l + 1) * block, :] for k in range(ny)], axis=0)
            for l in range(XL)
        ],
        axis=1,
    )
    turned = jnp.dot(turn, turned, preferred_element_type=F32).astype(BF16)
    for l in range(XL):
        x_out[l] = turned[:, l * LANES : (l + 1) * LANES]

    @pl.loop(1, nx)
    def _(d):
        other = (x + d) % nx
        target = to(other // XL * nz + z, y * XL + other % XL, t)
        remote(x_out.at[other % XL], rows.at[z, t, x], 3, x_sem, target).start()

    kept = pltpu.make_async_copy(x_out.at[xl], rows.at[z, t, x], local_sem.at[2])
    kept.start()
    send_weights(nz * nt, nr * nt)

    @pl.loop(1, nr)
    def _(d):
        other = (r + d) % nr
        remote(meta.at[r], meta.at[r], 1, meta_sem, to(other, e, t)).start()

    steps, heads, full = queries.shape
    positions = cache.shape[1]

    def score():
        scores[...] = jnp.dot(
            queries[...].reshape(steps * heads, full), cache[...], preferred_element_type=F32
        )

    def attend(s):
        position = iota((1, positions), 1)
        seen = jnp.where(
            position < lengths[0] + s + 1, scores[s * heads : (s + 1) * heads] * SCORE_SCALE, -jnp.inf
        )
        raised = jnp.exp(seen - jnp.max(seen, axis=-1, keepdims=True))
        shares = raised * (1.0 / jnp.sum(raised, axis=-1, keepdims=True))
        att[s] = lax.dot_general(
            shares.astype(BF16), cache[: full - ROPE, :], (((1,), (1,)), ((), ())),
            preferred_element_type=F32,
        ).astype(BF16)

    def permute():
        size = per * chunk_rows
        out_row, in_row = iota((size, 1), 0), iota((size, size), 1)
        home, rest = out_row >> log2(piece), out_row & (piece - 1)
        source = (
            (rest >> log2(XH * SLOTS)) * chunk_rows
            + (((rest >> log2(SLOTS)) & (XH - 1)) * XL + (home & (XL - 1))) * line_rows
            + (home >> log2(XL)) * SLOTS
            + (rest & (SLOTS - 1))
        )
        perm[...] = onehot(source == in_row)

    def homes(group):
        for index in range(group * per, (group + 1) * per):
            for h in range(XH):
                yield index - group * per, h, h * nz + (z + order[index] + nz) % nz

    def prepare(group):
        position = iota((tok, ne * piece), 1).astype(F32)
        for index, h, home in homes(group):
            facts = meta[home]
            for k in range(2):
                start = ((index * XH + h) * 2 + k) * tok
                place = facts[:, k : k + 1] + (index * XH + h) * SLOTS
                pick[group, start : start + tok, :] = onehot(position == place)
                gains[group, start : start + tok, :] = facts[:, 2 + k : 3 + k]

    hx = nx // 2

    def piece_of(offset, h):
        return rows.at[(z + offset + nz) % nz, t, pl.ds(h * hx, hx)]

    def ring(offset, h, sem, direction):
        target = to(xh * nz + (z + direction + nz) % nz, e, t)
        return remote(piece_of(offset, h), piece_of(offset, h), 4, sem, target)

    def pair(index, h):
        ref = piece_of(order[index], h)
        return remote(ref, ref, 5, pair_sem.at[index, h], to(r, e, 1 - t))

    def product(first, end):
        for index in range(first, end):
            for h in range(2):
                pair(index, h).wait_recv()
        lefts = []
        for index in range(first, end):
            chunk = rows.at[(z + order[index] + nz) % nz]
            lefts.append(
                jnp.concatenate(
                    [
                        chunk[u, :, c * line_rows : (c + 1) * line_rows, :].reshape(chunk_rows, LANES)
                        for u in range(nt)
                        for c in range(chunks)
                    ],
                    axis=1,
                )
            )
        value = lax.dot_general(
            jnp.concatenate(lefts, axis=0), wfull[...], (((1,), (1,)), ((), ())),
            preferred_element_type=F32,
        ).astype(BF16)
        where = first % per * chunk_rows
        products[where : where + (end - first) * chunk_rows, :width] = value

    def unpack():
        mine.wait()
        settle(pack_in.at[pl.ds(0, nr * nt - 1)], w_sem)

        @pl.loop(0, nr)
        def _(s):
            values = [pack_in[s * nt + u] for u in range(nt)]
            for g in range(2):
                wfull[high * g : high * (g + 1), pl.ds(pl.multiple_of(s * nt * depth, nt * depth), nt * depth)] = (
                    jnp.concatenate([v[:, depth * g : depth * (g + 1)] for v in values], axis=1)
                )

    def send_back(group):
        value = jnp.dot(perm[...], products[...], preferred_element_type=F32).astype(BF16)
        for g in range(halves):
            r_out[group, :, g * piece : (g + 1) * piece, :] = value[:, g * LANES : (g + 1) * LANES].reshape(
                ne, piece, LANES
            )

        @pl.loop(1, ne)
        def _(d):
            other = (e + d) % ne
            remote(r_out.at[group, other], r_in.at[group, e], 6, r_sem.at[group], to(r, other, t)).start()

        here = pltpu.make_async_copy(r_out.at[group, e], r_in.at[group, e], local_sem.at[5])
        here.start()
        here.wait()

    def combine(group):
        settle(r_in.at[group, pl.ds(0, ne - 1)], r_sem.at[group])
        arrived = r_in[group]
        arrived = jnp.concatenate(
            [arrived[:, g * piece : (g + 1) * piece, :].reshape(ne * piece, LANES) for g in range(halves)], axis=1
        )
        picked = jnp.dot(pick[group], arrived, preferred_element_type=F32) * gains[group]
        for index, h, home in homes(group):
            start = (index * XH + h) * 2 * tok
            f_out[home] = (picked[start : start + tok] + picked[start + tok : start + 2 * tok]).astype(BF16)
        for index, h, home in homes(group):
            if group == 0 and index == 0:
                @pl.when(h == xh)
                def _():
                    f_in[home] = f_out[home]

                @pl.when(h != xh)
                def _():
                    remote(f_out.at[home], f_in.at[r], 7, f_sem, to(home, e, t)).start()
            else:
                remote(f_out.at[home], f_in.at[r], 7, f_sem, to(home, e, t)).start()

    last = nz // 2

    def when(index):
        return min(last, max(2, (index + 1) // 2))

    def forward(step):
        for h in range(2):
            if step == 0:
                ring(0, h, right_sem.at[0, h], 1).start()
                ring(0, h, left_sem.at[0, h], -1).start()
                pair(0, h).start()
                continue
            if step < last or h == 0:
                ring(-step, h, right_sem.at[step - 1, h], 1).wait_recv()
                if step + 1 < last or (step + 1 == last and h == 0):
                    ring(-step, h, right_sem.at[step, h], 1).start()
                pair(2 * step - 1, h).start()
            if step < last or h == 1:
                ring(step, h, left_sem.at[step - 1, h], -1).wait_recv()
                if step + 1 < last or (step + 1 == last and h == 1):
                    ring(step, h, left_sem.at[step, h], -1).start()
                pair(2 * step if step < last else 2 * step - 1, h).start()

    score()
    kept.wait()
    settle(rows.at[0, 0, pl.ds(0, nx - 1)], x_sem)
    forward(0)
    for s in range(steps):
        attend(s)
    attended_copy = pltpu.make_async_copy(att, attended, local_sem.at[3])
    attended_copy.start()
    permute()
    settle(meta.at[pl.ds(0, nr - 1)], meta_sem)
    for group in range(groups):
        prepare(group)
    products[...] = jnp.zeros_like(products)
    for step in range(1, last + 1):
        forward(step)
        if step == min(2, last):
            unpack()
            synced_copy = pltpu.make_async_copy(wfull, synced, local_sem.at[4])
            synced_copy.start()
        for group in range(groups):
            first, end = group * per, (group + 1) * per
            if step == when(end - 1):
                if first < end - 1 and step > when(end - 2):
                    product(end - 1, end)
                else:
                    product(first, end)
                send_back(group)
            elif step == when(end - 2):
                product(first, end - 1)
        if step == last - 1:
            for group in range(groups - 3):
                combine(group)
    for group in range(max(0, groups - 3), groups):
        combine(group)

    settle(y_out.at[pl.ds(0, ny - 1)], send_sem.at[0])
    settle(meta.at[pl.ds(0, nr - 1)], send_sem.at[1])
    settle(pack_out.at[pl.ds(0, nr * nt - 1)], send_sem.at[2])
    settle(rows.at[0, 0, pl.ds(0, nx - 1)], send_sem.at[3])
    settle(rows.at[pl.ds(0, nz - 1), 0], send_sem.at[4])
    settle(rows.at[:, 0], send_sem.at[5])
    for group in range(groups):
        settle(r_out.at[group, pl.ds(0, ne - 1)], send_sem.at[6])
    settle(f_out.at[pl.ds(0, nr - 1)], send_sem.at[7])
    attended_copy.wait()
    synced_copy.wait()
    settle(f_in.at[pl.ds(0, nr - 1)], f_sem)
    size = nr * tok
    out_row, in_row = iota((size, 1), 0), iota((size, size), 1)
    source = (out_row & (nr - 1)) * tok + (out_row >> log2(nr))
    value = jnp.dot(
        onehot(source == in_row), f_in[...].reshape(size, f_in.shape[2]), preferred_element_type=F32
    )
    final[...] = value[:, :width].astype(BF16).reshape(tok, nr, width)
    result = pltpu.make_async_copy(final, gathered, local_sem.at[1])
    result.start()
    result.wait()


def local(sizes, queries, latent_cache, cache_lengths, hidden_acts, routes, route_weights, stored_values, block_scales):
    nr, ne, nt = sizes
    nz, ny, nx = nr // XH, ne // XL, XH * XL
    steps, _, heads, full = queries.shape
    tok, _, ffn = hidden_acts.shape
    depth, columns = stored_values.shape[1:]
    width = columns // (nr * nt)
    padded = -(-width // LANES) * LANES
    chunks = ffn // (nt * LANES)
    block = chunks * SLOTS
    groups = nz // PER
    per = PER
    piece = per * XH * SLOTS
    size = nx * ny * SLOTS
    vmem = pl.BlockSpec(memory_space=pltpu.VMEM)
    smem = pl.BlockSpec(memory_space=pltpu.SMEM)
    hbm = pl.BlockSpec(memory_space=pl.ANY)
    dma = pltpu.SemaphoreType.DMA
    attended, synced, gathered = pl.pallas_call(
        functools.partial(kernel, sizes),
        out_shape=[
            jax.ShapeDtypeStruct((steps, heads, full - ROPE), BF16),
            jax.ShapeDtypeStruct((width, ffn), BF16),
            jax.ShapeDtypeStruct((tok, nr, width), BF16),
        ],
        in_specs=[smem, smem, vmem, vmem, vmem, vmem, vmem, vmem],
        out_specs=[hbm, hbm, hbm],
        scratch_shapes=[
            pltpu.VMEM((nr * nt, width // 2, 2 * depth), BF16),
            pltpu.VMEM((nr * nt, width // 2, 2 * depth), BF16),
            pltpu.VMEM((width, ffn), BF16),
            pltpu.VMEM((chunks * 2 * tok, LANES), BF16),
            pltpu.VMEM((ny, XL * block, LANES), BF16),
            pltpu.VMEM((ny, XL * block, LANES), BF16),
            pltpu.VMEM((XL, ny * block, LANES), BF16),
            pltpu.VMEM((nz, nt, nx, ny * block, LANES), BF16),
            pltpu.VMEM((per * size, padded), BF16),
            pltpu.VMEM((groups, ne, piece * (padded // LANES), LANES), BF16),
            pltpu.VMEM((groups, ne, piece * (padded // LANES), LANES), BF16),
            pltpu.VMEM((nr, tok, LANES), F32),
            pltpu.VMEM((groups, per * XH * 2 * tok, ne * piece), BF16),
            pltpu.VMEM((groups, per * XH * 2 * tok, 1), F32),
            pltpu.VMEM((nr, tok, padded), BF16),
            pltpu.VMEM((nr, tok, padded), BF16),
            pltpu.VMEM((tok, nr, width), BF16),
            pltpu.VMEM((per * size, per * size), BF16),
            pltpu.VMEM((steps * heads, latent_cache.shape[1]), F32),
            pltpu.VMEM((steps, heads, full - ROPE), BF16),
            dma((6,)),
            dma((8,)),
            dma,
            dma,
            dma,
            dma((nz // 2, 2)),
            dma((nz // 2, 2)),
            dma((nz, 2)),
            dma,
            dma((groups,)),
            dma,
        ],
        compiler_params=pltpu.CompilerParams(
            collective_id=0, has_side_effects=True, vmem_limit_bytes=56 * 1024 * 1024
        ),
        cost_estimate=pl.CostEstimate(flops=2_000_000_000, bytes_accessed=6_000_000, transcendentals=262144),
    )(
        cache_lengths,
        block_scales[0],
        routes.T,
        route_weights.T,
        hidden_acts,
        queries.reshape(steps, heads, full),
        latent_cache[0].T,
        stored_values[0],
    )
    expert_output = gathered.reshape(tok, nr, 1, width)
    return attended.reshape(steps, 1, heads, full - ROPE), synced.T[None], expert_output


def solution(mesh):
    sizes = (mesh.shape["replica"], mesh.shape["expert"], mesh.shape["tensor"])
    placed = (
        P(None, ("replica", "expert"), "tensor", None),
        P(("replica", "expert"), None, None),
        P(("replica", "expert")),
        P(("replica", "expert"), None, None),
        P(("replica", "expert"), None),
        P(("replica", "expert"), None),
        P("expert", ("replica", "tensor"), None),
        P("expert", None, None),
    )
    return jax.shard_map(
        functools.partial(local, sizes),
        mesh=mesh,
        in_specs=placed,
        out_specs=(
            P(None, ("replica", "expert"), "tensor", None),
            P("expert", None, ("replica", "tensor")),
            P(("replica", "expert"), None, "tensor", None),
        ),
        check_vma=False,
    )
```

time: 116 us -> 110 us (0.948)
  local copies, waits for them, and re-layouts: 10.4 us -> 4.56 us
    unnamed x11 -> x5, local copies, waits for them, and re-layouts: 10.4 us -> 4.56 us
where the time goes in v2:
time: 110 us
  Pallas kernels  104 us (95%)
  local copies, waits for them, and re-layouts  4.56 us (4%)
  between operations  1.3 us (1%)
    pallas_call x1, Pallas kernels, local(): pl.pallas_call(functools.partial(kernel, sizes), out_shape=[jax.ShapeDtyp...  104 us
    unnamed x5, local copies, waits for them, and re-layouts  4.56 us

profile of v2, /device:TPU:1, one launch (start us, length us, event | category | flops | bytes accessed | tf_op | source)
XLA Modules:
  0.0 110.2 jit_solution(13116466733999919)
XLA Ops:
  1.3 104.4 %shard_map.103 = (bf16[4,64,512]{2,1,0:T(8,128)(2,1)}, bf16[224,2048]{1,0:T(8,128)(2,1)}, bf16[16,16,224]{2,1,0:T(8,128)(2,1)}) custom-call(s32[1]{0:T(128)S(6)} %copy.16.lengths, f32[16,56]{1,0:T(8,128)} %bitcast.23, s32[2,16]{1,0:T(2,128)} %bitcast.24, f32[2,16]{1,0:T(2,128)} %bitcast.25, bf16[16,2,2048]{2,1,0:T(2,128)(2,1)} %hidden.1, ...), custom_call_target="tpu_custom_call" | custom-call | flops 2000000000 | bytes 6000000 | tf_op jit(solution)/shard_map/pallas_call | solution.py:477
  105.6 0.0 copy-start
  105.7 1.7 %copy.17 = bf16[4,1,64,512]{3,2,1,0:T(8,128)(2,1)} copy(bf16[4,1,64,512]{3,2,1,0:T(8,128)(2,1)} %bitcast.18) | data formatting | bytes 524288
  107.4 2.2 %copy.18 = bf16[1,2048,224]{1,2,0:T(8,128)(2,1)} copy(bf16[1,2048,224]{1,2,0:T(8,128)(2,1)} %bitcast.17) | data formatting | bytes 1835008
  109.6 0.0 copy-done
  109.6 0.7 copy.19
Async XLA Ops:
  105.6 3.9 %copy-start = (bf16[16,16,224]{2,1,0:T(8,128)(2,1)S(1)}, bf16[16,16,224]{2,1,0:T(8,128)(2,1)}, u32[]{:S(2)}) copy-start(bf16[16,16,224]{2,1,0:T(8,128)(2,1)} %get-tuple-element.8) | copy-start | bytes 344068

commit v3 on v2

--- a/solution.py
+++ b/solution.py
@@ -14,7 +14,8 @@
 ROPE = 64
 SCORE_SCALE = 192.0 ** (-0.5)
 LANES = 128
-PER = 2
+WAVES = (7, 12, 12, 0)
+PER = 4
 MESH = pl.DeviceIdType.MESH
 F32 = jnp.float32
 BF16 = jnp.bfloat16
@@ -200,7 +201,11 @@
             other = (me + d) % (nz * nt) + (xh + d // (nz * nt)) % XH * (nz * nt)
             remote(pack_out.at[other], pack_in.at[me], 2, w_sem, to(other // nt, e, other % nt)).start()
 
-    send_weights(1, nz * nt)
+    cuts = [1]
+    for wave in WAVES:
+        cuts.append(min(nr * nt, cuts[-1] + wave))
+    cuts[-1] = nr * nt
+    send_weights(cuts[0], cuts[1])
     mine = pltpu.make_async_copy(pack_out.at[me], pack_in.at[me], local_sem.at[1])
     mine.start()
 
@@ -233,7 +238,7 @@
 
     kept = pltpu.make_async_copy(x_out.at[xl], rows.at[z, t, x], local_sem.at[2])
     kept.start()
-    send_weights(nz * nt, nr * nt)
+    send_weights(cuts[1], cuts[2])
 
     @pl.loop(1, nr)
     def _(d):
@@ -401,6 +406,7 @@
     kept.wait()
     settle(rows.at[0, 0, pl.ds(0, nx - 1)], x_sem)
     forward(0)
+    send_weights(cuts[2], cuts[3])
     for s in range(steps):
         attend(s)
     attended_copy = pltpu.make_async_copy(att, attended, local_sem.at[3])
@@ -410,8 +416,11 @@
     for group in range(groups):
         prepare(group)
     products[...] = jnp.zeros_like(products)
+    early = 0
     for step in range(1, last + 1):
         forward(step)
+        if step == 1:
+            send_weights(cuts[3], cuts[4])
         if step == min(2, last):
             unpack()
             synced_copy = pltpu.make_async_copy(wfull, synced, local_sem.at[4])
@@ -426,10 +435,10 @@
                 send_back(group)
             elif step == when(end - 2):
                 product(first, end - 1)
-        if step == last - 1:
-            for group in range(groups - 3):
-                combine(group)
-    for group in range(max(0, groups - 3), groups):
+        if step == last - 1 and groups > 1 and when(per - 1) <= step:
+            combine(0)
+            early = 1
+    for group in range(early, groups):
         combine(group)
 
     settle(y_out.at[pl.ds(0, ny - 1)], send_sem.at[0])
@@ -454,6 +463,20 @@
     result = pltpu.make_async_copy(final, gathered, local_sem.at[1])
     result.start()
     result.wait()
+
+
+def write_results(a, b, c, a_out, b_out, c_out, sem):
+    parts = 4
+    rows = b.shape[0] // parts
+    copies = [pltpu.make_async_copy(a, a_out, sem.at[0]), pltpu.make_async_copy(c, c_out, sem.at[1])]
+    for k in range(parts):
+        copies.append(
+            pltpu.make_async_copy(b.at[pl.ds(k * rows, rows)], b_out.at[pl.ds(k * rows, rows)], sem.at[2 + k])
+        )
+    for copy in copies:
+        copy.start()
+    for copy in copies:
+        copy.wait()
 
 
 def local(sizes, queries, latent_cache, cache_lengths, hidden_acts, routes, route_weights, stored_values, block_scales):
@@ -530,6 +553,14 @@
         latent_cache[0].T,
         stored_values[0],
     )
+    results = [attended, synced, gathered]
+    attended, synced, gathered = pl.pallas_call(
+        write_results,
+        out_shape=[jax.ShapeDtypeStruct(v.shape, v.dtype) for v in results],
+        in_specs=[hbm] * 3,
+        out_specs=[hbm] * 3,
+        scratch_shapes=[dma((6,))],
+    )(*results)
     expert_output = gathered.reshape(tok, nr, 1, width)
     return attended.reshape(steps, 1, heads, full - ROPE), synced.T[None], expert_output
 

time: 110 us -> 148 us (1.35)
  Pallas kernels: 104 us -> 146 us
  local copies, waits for them, and re-layouts: 4.56 us -> 0 us
    pallas_call x0 -> x1, Pallas kernels: none -> 40.9 us  [local(): pl.pallas_call(write_results, out_shape=[jax.ShapeDtypeStruct(v.shape, v....]
    unnamed x5 -> x0, local copies, waits for them, and re-layouts: 4.56 us -> none
where the time goes in v3:
time: 148 us; the launch traced here: 147 us
  Pallas kernels  146 us (99%)
    pallas_call x1, Pallas kernels, local(): pl.pallas_call(functools.partial(kernel, sizes), out_shape=[jax.ShapeDtyp...  105 us
    pallas_call x1, Pallas kernels, local(): pl.pallas_call(write_results, out_shape=[jax.ShapeDtypeStruct(v.shape, v....  40.9 us

profile of v3, /device:TPU:1, one launch (start us, length us, event | category | flops | bytes accessed | tf_op | source)
XLA Modules:
  0.0 147.5 jit_solution(14576867894479307300)
XLA Ops:
  1.3 105.3 %shard_map.103 = (bf16[4,64,512]{2,1,0:T(8,128)(2,1)}, bf16[224,2048]{1,0:T(8,128)(2,1)}, bf16[16,16,224]{2,1,0:T(8,128)(2,1)}) custom-call(s32[1]{0:T(128)S(6)} %copy.13.lengths, f32[16,56]{1,0:T(8,128)} %bitcast.23, s32[2,16]{1,0:T(2,128)} %bitcast.24, f32[2,16]{1,0:T(2,128)} %bitcast.25, bf16[16,2,2048]{2,1,0:T(2,128)(2,1)} %hidden.1, ...), custom_call_target="tpu_custom_call" | custom-call | flops 2000000000 | bytes 6000000 | tf_op jit(solution)/shard_map/pallas_call | solution.py:500
  106.6 40.9 %shard_map.104 = (bf16[4,64,512]{2,1,0:T(8,128)(2,1)}, bf16[224,2048]{1,0:T(8,128)(2,1)}, bf16[16,16,224]{2,1,0:T(8,128)(2,1)}) custom-call(bf16[4,64,512]{2,1,0:T(8,128)(2,1)} %get-tuple-element.9.a, bf16[224,2048]{1,0:T(8,128)(2,1)} %get-tuple-element.10.b, bf16[16,16,224]{2,1,0:T(8,128)(2,1)} %get-tuple-element.11.c), custom_call_target="tpu_custom_call" | custom-call | tf_op jit(solution)/shard_map/pallas_call | solution.py:557
